TPU v7x, 512 devices: a whole 4x8x8 slice. The times are simulated.
512 devices in a mesh: row: 64 (over y_lo, z, core), col: 8 (over y_hi, x).
Axes of the slice: x: 4, y: 8 (y_hi: 2, y_lo: 4; y = y_hi * 4 + y_lo), z: 8, core: 2. Of those that a mesh axis runs over, the one named last changes fastest.
Arguments:
- vectors: float32 [32768, 1024], P('row', 'col'), may hold values from -6 to 6
- householder: float32 [2, 32768, 256], P(None, 'row', 'col'), may hold values from -0.03125 to 0.03125
- tfactors: float32 [2, 256, 256], P(None, None, 'col'), may hold values from -0.17 to 2, as said below
Outputs:
- transformed: float32 [32768, 1024], P('row', 'col')
Inputs may be any that keep to these rules, and one draw needn't show every extreme that they name: Each tfactors[b] is upper triangular with a positive diagonal between 1 and 2.
All inputs are finite; a program needn't handle non-finite values.
Results may differ from a plain program's by a relative error of at most 0.0001.
Values sent between devices are 32-bit elements; how exact they have to be, the bound alone decides.
A program may use at most 64 MiB of HBM per device.

v0:
```python
import jax
import jax.numpy as jnp
from jax import lax
from jax.sharding import PartitionSpec as P

BLOCKS = 2


def turned_gather(arrays, axis, dims):
    turned = [jnp.moveaxis(a, dim, 0) for a, dim in zip(arrays, dims)]
    both = jnp.concatenate([t.reshape(len(t), -1) for t in turned], axis=1)
    whole, at, finished = (lax.all_gather(both, axis, axis=0, tiled=True), 0, [])
    for t, dim in zip(turned, dims):
        section = whole[:, at : at + t[0].size].reshape(-1, *t.shape[1:])
        finished.append(jnp.moveaxis(section, 0, dim))
        at += t[0].size
    return tuple(finished)


def split_up(value, dim, length):
    before, after = (value.shape[:dim], value.shape[dim + 1 :])
    return jnp.moveaxis(value.reshape(*before, length, -1, *after), dim, 0)


def summed_on_arrival(value, axis, dim):
    length = lax.axis_size(axis)
    tiles = lax.all_to_all(split_up(value, dim, length), axis, 0, 0, tiled=True)
    return jnp.sum(tiles, axis=0)


def joined_along(tiles, dim):
    lengths = list(tiles.shape[1:])
    lengths[dim] *= tiles.shape[0]
    return jnp.moveaxis(tiles, 0, dim).reshape(lengths)


def copy_for_each(value, axis):
    copies = jnp.broadcast_to(value, (lax.axis_size(axis), *value.shape))
    return lax.all_to_all(copies, axis, split_axis=0, concat_axis=0, tiled=True)


def collect(value, axis, dim):
    return joined_along(copy_for_each(value, axis), dim)


def project(current, blockv):
    return lax.dot_general(
        current,
        blockv,
        (((0,), (0,)), ((), ())),
        precision=lax.Precision.HIGHEST,
        preferred_element_type=jnp.float32,
    )


def apply_factor(products_t, blockt):
    return lax.dot_general(
        products_t,
        blockt,
        (((1,), (1,)), ((), ())),
        precision=lax.Precision.HIGHEST,
        preferred_element_type=jnp.float32,
    )


def on_device(vectors, householder, tfactors):
    current = vectors
    for block in range(BLOCKS):
        blockv, blockt = turned_gather((householder[block], tfactors[block]), "col", (1, 1))
        source = current
        shares = summed_on_arrival(project(source, blockv), "row", 0)
        reflect_share = apply_factor(shares, blockt)
        reflect_t = collect(reflect_share, "row", 0)
        current = current - lax.dot_general(
            blockv,
            reflect_t,
            (((1,), (1,)), ((), ())),
            precision=lax.Precision.HIGHEST,
            preferred_element_type=jnp.float32,
        )
    return current


def solution(mesh):
    return jax.shard_map(
        on_device,
        mesh=mesh,
        in_specs=(P("row", "col"), P(None, "row", "col"), P(None, None, "col")),
        out_specs=P("row", "col"),
        check_vma=False,
    )
```

profile of v0, /device:TPU:1, one launch (start us, length us, event | category | flops | bytes accessed | tf_op | source)
XLA Modules:
  0.0 163.8 jit_solution(3380706604660088206)
XLA Ops:
  0.0 0.0 copy-start.1
  0.0 0.8 slice_bitcast_fusion.2
  0.8 0.1 copy-done.1
  1.0 0.0 copy-start
  1.0 45.1 %all_gather.6 = f32[256,768]{1,0:T(8,128)S(1)} all-gather(f32[32,768]{1,0:T(8,128)S(1)} %pad_maximum_fusion), channel_id=1, replica_groups=mesh['row'=64,'col'=8] {'col'}, dimensions={0}, use_global_device_ids=true | all-gather | bytes 884736 | tf_op jit(solution)/shard_map/all_gather | solution.py:12
  46.1 0.0 copy-done
  46.1 0.6 convolution_bitcast_fusion
  46.7 0.7 reshape.12
  47.5 15.6 %all-to-all-start = ((f32[64,2,256]{2,1,0:T(2,128)}), f32[64,2,256]{2,1,0:T(2,128)S(1)}, u32[]{:S(2)}, u32[]{:S(2)}) async-start(f32[64,2,256]{2,1,0:T(2,128)} %reshape.12), calls=%async_computation | async-start | bytes 262144 | tf_op jit(solution)/shard_map/all_to_all | solution.py:27
  63.1 10.0 %all-to-all-done = f32[64,2,256]{2,1,0:T(2,128)S(1)} async-done(((f32[64,2,256]{2,1,0:T(2,128)}), f32[64,2,256]{2,1,0:T(2,128)S(1)}, u32[]{:S(2)}, u32[]{:S(2)}) %all-to-all-start) | async-done | bytes 131104 | tf_op jit(solution)/shard_map/all_to_all | solution.py:27
  73.0 0.1 reduce_sum.18
  73.1 0.2 fusion.7
  73.3 0.7 broadcast_in_dim.6
  74.0 5.0 %all-to-all-start.1 = ((f32[64,2,256]{2,1,0:T(2,128)}), f32[64,2,256]{2,1,0:T(2,128)S(1)}, u32[]{:S(2)}, u32[]{:S(2)}) async-start(f32[64,2,256]{2,1,0:T(2,128)} %broadcast_in_dim.6), calls=%async_computation.1 | async-start | bytes 262144 | tf_op jit(solution)/shard_map/all_to_all | solution.py:39
  79.0 40.2 %all_gather.7 = f32[256,768]{1,0:T(8,128)S(1)} all-gather(f32[32,768]{1,0:T(8,128)S(1)} %pad_maximum_fusion.1), channel_id=1, replica_groups=mesh['row'=64,'col'=8] {'col'}, dimensions={0}, use_global_device_ids=true | all-gather | bytes 884736 | tf_op jit(solution)/shard_map/all_gather | solution.py:12
  119.2 0.0 all-to-all-done.1
  119.2 0.1 reshape.13
  119.3 1.0 convolution_subtract_fusion.1
  120.3 0.6 fusion.1
  120.9 0.1 reshape.14
  121.0 26.1 %all_to_all.20 = f32[64,2,256]{2,1,0:T(2,128)S(1)} all-to-all(f32[64,2,256]{2,1,0:T(2,128)S(1)} %reshape.14), channel_id=1, replica_groups=mesh['row'=64,'col'=8] {'row'}, dimensions={0} | all-to-all | bytes 262144 | tf_op jit(solution)/shard_map/all_to_all | solution.py:27
  147.1 0.1 reduce_sum.19
  147.1 0.2 fusion.5
  147.3 0.1 broadcast_in_dim.7
  147.4 14.6 %all_to_all.21 = f32[64,2,256]{2,1,0:T(2,128)S(1)} all-to-all(f32[64,2,256]{2,1,0:T(2,128)S(1)} %broadcast_in_dim.7), channel_id=1, replica_groups=mesh['row'=64,'col'=8] {'row'}, dimensions={0} | all-to-all | bytes 262144 | tf_op jit(solution)/shard_map/all_to_all | solution.py:39
  162.0 0.1 reshape.15
  162.1 1.7 %convolution_subtract_fusion = f32[512,128]{1,0:T(8,128)} fusion(f32[512,128]{1,0:T(8,128)S(1)} %convolution_subtract_fusion.1, f32[128,256]{1,0:T(8,128)S(1)} %reshape.15, f32[256,768]{1,0:T(8,128)S(1)} %all_gather.7), kind=kOutput, calls=%fused_computation | convolution fusion | flops 201392128 | bytes 1179648 | tf_op jit(solution)/shard_map/dot_general | solution.py:74
  (3 shorter events, 0.0 us)
Async XLA Ops:
  0.0 0.9 copy-start.1
  1.0 45.2 %copy-start = (f32[512,128]{1,0:T(8,128)S(1)}, f32[512,128]{1,0:T(8,128)}, u32[]{:S(2)}) copy-start(f32[512,128]{1,0:T(8,128)} %param.3) | copy-start | bytes 786436
  47.5 25.6 %all-to-all-start = ((f32[64,2,256]{2,1,0:T(2,128)}), f32[64,2,256]{2,1,0:T(2,128)S(1)}, u32[]{:S(2)}, u32[]{:S(2)}) async-start(f32[64,2,256]{2,1,0:T(2,128)} %reshape.12), calls=%async_computation | async-start | bytes 262144 | tf_op jit(solution)/shard_map/all_to_all | solution.py:27
  74.0 45.2 %all-to-all-start.1 = ((f32[64,2,256]{2,1,0:T(2,128)}), f32[64,2,256]{2,1,0:T(2,128)S(1)}, u32[]{:S(2)}, u32[]{:S(2)}) async-start(f32[64,2,256]{2,1,0:T(2,128)} %broadcast_in_dim.6), calls=%async_computation.1 | async-start | bytes 262144 | tf_op jit(solution)/shard_map/all_to_all | solution.py:39
where the time goes:
time: 164 us
  blocking collectives  126 us (77%)
  starting transfers between devices  20.6 us (13%)
  waiting for transfers between devices  9.97 us (6%)
  matrix products  4.25 us (3%)
  local copies, waits for them, and re-layouts  2.75 us (2%)
    all_gather x2, blocking collectives, turned_gather(): lax.all_gather(both, axis, axis=0, tiled=True)  85.3 us
    all_to_all x1, blocking collectives, summed_on_arrival(): tiles = lax.all_to_all(split_up(value, dim, length), axis, 0, 0, tiled=True)  26.1 us
    all_to_all x1, starting transfers between devices, summed_on_arrival(): tiles = lax.all_to_all(split_up(value, dim, length), axis, 0, 0, tiled=True)  15.6 us
    all_to_all x1, blocking collectives, copy_for_each(): return lax.all_to_all(copies, axis, split_axis=0, concat_axis=0, tiled=True)  14.6 us
    all_to_all x1, waiting for transfers between devices, summed_on_arrival(): tiles = lax.all_to_all(split_up(value, dim, length), axis, 0, 0, tiled=True)  9.97 us
    all_to_all x1, starting transfers between devices, copy_for_each(): return lax.all_to_all(copies, axis, split_axis=0, concat_axis=0, tiled=True)  4.96 us
  transfers between devices with their start and end apart: 2, of which 1 were waited for; matrix products, arithmetic and copies ran while one was open for 0% of the time, Pallas kernels for 0%

commit v1 on v0

v1 whole, which is shorter than its diff:
```python
import functools

import jax
import jax.numpy as jnp
from jax import lax
from jax.experimental import pallas as pl
from jax.experimental.pallas import tpu as pltpu
from jax.sharding import PartitionSpec as P

MESH = pl.DeviceIdType.MESH
F32 = jnp.float32
BF16 = jnp.bfloat16
YL, NZ, CORES = 4, 8, 2
YH, NX = 2, 4
NT = (((1,), (1,)), ((), ()))
NN = (((1,), (0,)), ((), ()))


def split(value):
    high = value.astype(BF16)
    return high, (value - high.astype(F32)).astype(BF16)


def dot3(a, b, dims):
    def one(left, right):
        return lax.dot_general(left, right, dims, preferred_element_type=F32)

    return one(a[0], b[0]) + (one(a[0], b[1]) + one(a[1], b[0]))


class Copies:
    def __init__(self, send, recv):
        self.send, self.recv, self.used, self.open = send, recv, 0, []

    def start(self, src, dst, device):
        at = self.used
        self.used += 1
        copy = pltpu.make_async_remote_copy(
            src_ref=src,
            dst_ref=dst,
            send_sem=self.send.at[at],
            recv_sem=self.recv.at[at],
            device_id=device,
            device_id_type=MESH,
        )
        copy.start()
        self.open.append(copy)
        return copy

    def finish(self):
        for copy in self.open:
            copy.wait_send()


N_COPIES = 2 * 7 + 7 + 2 * (1 + 3 + 7 + 3 + 4) + 31 + 1


def kernel(
    v_in, t_in, c_in, out_ref,
    vt, tt, c_v, lhs_h, lhs_l,
    pp0, pp1, cr0, cr1, s10, s11, yr0, yr1, s20, s21, zr0, zr1, pf0, pf1, gf,
    w1h, w1l, v0h, v0l,
    local_sem, send_sem, recv_sem,
):
    row, col = lax.axis_index("row"), lax.axis_index("col")
    core, z, yl = lax.rem(row, 2), lax.rem(row // 2, NZ), row // (2 * NZ)
    x, yh = lax.rem(col, NX), col // NX

    def at(dc=0, dz=0, dyl=0, dx=0, dyh=0):
        r = (lax.rem(yl + dyl, YL) * NZ + lax.rem(z + dz, NZ)) * 2 + lax.rem(core + dc, 2)
        c = lax.rem(yh + dyh, YH) * NX + lax.rem(x + dx, NX)
        return (r, c)

    other_col = lax.rem(yh + 1, YH) * NX + x
    loads = [
        pltpu.make_async_copy(v_in.at[0], vt.at[0, col], local_sem.at[0]),
        pltpu.make_async_copy(v_in.at[1], vt.at[1, col], local_sem.at[1]),
        pltpu.make_async_copy(c_in, c_v, local_sem.at[2]),
        pltpu.make_async_copy(t_in, tt.at[col], local_sem.at[3]),
    ]
    for load in loads:
        load.start()

    barrier = pltpu.get_barrier_semaphore()
    partners = [at(dyh=1)]
    partners += [at(dz=d) for d in (4, 3, 5, 2, 6, 1, 7)]
    partners += [at(dyl=d) for d in (1, 2, 3)] + [at(dx=d) for d in (2, 1, 3)] + [at(dc=1)]
    for device in partners:
        pl.semaphore_signal(barrier, inc=1, device_id=device, device_id_type=MESH)
    loads[0].wait()
    loads[1].wait()
    pl.semaphore_wait(barrier, len(partners))

    copies = Copies(send_sem, recv_sem)

    def along_x(ref):
        return [copies.start(ref, ref, at(dx=d)) for d in (2, 1, 3)]

    v_own, v_far, v_far_x = [None] * 2, [None] * 2, [None] * 2
    for b in range(2):
        mine = vt.at[b, col]
        v_far[b] = copies.start(mine, mine, at(dyh=1))
        v_own[b] = along_x(mine)
    loads[3].wait()
    t_far = copies.start(tt.at[col], tt.at[col], at(dyh=1))

    loads[2].wait()
    for part in range(2):
        turned = jnp.transpose(c_v[pl.ds(256 * part, 256), :])
        high, low = split(turned)
        lhs_h[0:128, 256 * part : 256 * (part + 1)] = high
        lhs_l[0:128, 256 * part : 256 * (part + 1)] = low
    high, low = split(vt[1, col])
    lhs_h[128:160, :] = high
    lhs_l[128:160, :] = low

    for b in range(2):
        v_far[b].wait_recv()
        v_far_x[b] = along_x(vt.at[b, other_col])
    t_own = along_x(tt.at[col])
    t_far.wait_recv()
    t_far_x = along_x(tt.at[other_col])

    def project(b, half):
        rows = 160 if b == 0 else 128
        blockv = split(vt[b, pl.ds(half * NX, NX)].reshape(128, 512))
        value = dot3((lhs_h[0:rows, :], lhs_l[0:rows, :]), blockv, NT)
        pp = (pp0, pp1)[b]
        for h in range(2):
            for s in range(YL):
                first = 64 * h + 16 * s
                pp[h, s, pl.ds(2 * half, 2)] = value[first : first + 16].reshape(2, 8, 128)
        if b == 0:
            for s in range(YL):
                pp[half, s, 4] = value[128 + 8 * s : 136 + 8 * s]

    for b in range(2):
        for copy in v_own[b]:
            copy.wait_recv()
        project(b, yh)

    pps, crs, s1s, yrs, s2s, zrs, pfs = (
        (pp0, pp1), (cr0, cr1), (s10, s11), (yr0, yr1), (s20, s21), (zr0, zr1), (pf0, pf1),
    )
    across = [None] * 2
    for b in range(2):
        for copy in v_far_x[b]:
            copy.wait_recv()
        project(b, lax.rem(yh + 1, YH))
        across[b] = copies.start(pps[b].at[1 - core], crs[b], at(dc=1))

    down = [None] * 2
    for b in range(2):
        across[b].wait_recv()
        s1s[b][...] = pps[b][core] + crs[b][...]
        down[b] = [
            copies.start(s1s[b].at[lax.rem(yl + d, YL)], yrs[b].at[d - 1], at(dyl=d))
            for d in (3, 2, 1)
        ]

    around = [None] * 2
    for b in range(2):
        for copy in down[b]:
            copy.wait_recv()
        s2s[b][...] = s1s[b][yl] + yrs[b][0] + yrs[b][1] + yrs[b][2]
        around[b] = [
            copies.start(s2s[b], zrs[b].at[d - 1], at(dz=d)) for d in (4, 3, 5, 2, 6, 1, 7)
        ]

    for copy in t_own + t_far_x:
        copy.wait_recv()
    high, low = split(jnp.transpose(vt[0].reshape(256, 512)))
    v0h[...] = high
    v0l[...] = low
    t1 = split(tt[:, 1].reshape(256, 256))
    high, low = split(dot3(split(jnp.transpose(vt[1].reshape(256, 512))), t1, NT))
    w1h[...] = high
    w1l[...] = low

    up, over, g_out = [None] * 2, [None] * 2, []
    for b in range(2):
        for copy in around[b]:
            copy.wait_recv()
        total = s2s[b][...]
        for d in range(NZ - 1):
            total = total + zrs[b][d]
        mine = pfs[b].at[core, yl]
        mine[...] = total[0:4]
        if b == 0:
            gf[core, col, yl] = total[4]
        up[b] = [copies.start(mine, mine, at(dyl=d)) for d in (3, 2, 1)]
        over[b] = [copies.start(mine, mine, at(dc=1))]
        if b == 0:
            tile = gf.at[core, col, yl]
            for dyh in (1, 0):
                for dx in (2, 1, 3, 0):
                    for dyl in (3, 2, 1, 0):
                        if dyh or dx or dyl:
                            g_out.append(copies.start(tile, tile, at(dyl=dyl, dx=dx, dyh=dyh)))

    for b in range(2):
        for d, copy in zip((3, 2, 1), up[b]):
            copy.wait_recv()
            came = pfs[b].at[core, lax.rem(yl + YL - d, YL)]
            over[b].append(copies.start(came, came, at(dc=1)))

    def products(b):
        for copy in over[b]:
            copy.wait_recv()
        pf = pfs[b]
        left = pf[:, :, 0:2].reshape(128, 128)
        right = pf[:, :, 2:4].reshape(128, 128)
        return jnp.concatenate([left, right], axis=1)

    r0 = split(dot3(split(products(0)), split(tt[:, 0].reshape(256, 256)), NN))
    c_v[...] = c_v[...] - dot3((v0h[...], v0l[...]), r0, NT)

    for copy in g_out:
        copy.wait_recv()
    g_over = copies.start(gf.at[core], gf.at[core], at(dc=1))
    g_over.wait_recv()
    gram = jnp.concatenate([gf[0].reshape(256, 128), gf[1].reshape(256, 128)], axis=1)
    moved = dot3(r0, split(gram), NT)
    rest = split(products(1) - moved)
    out_ref[...] = c_v[...] - dot3((w1h[...], w1l[...]), rest, NT)
    copies.finish()


def on_device(vectors, householder, tfactors):
    v_t = jnp.swapaxes(householder, 1, 2)
    t_t = jnp.swapaxes(tfactors, 1, 2)
    any_spec = pl.BlockSpec(memory_space=pl.ANY)
    vmem = pltpu.VMEM
    return pl.pallas_call(
        kernel,
        out_shape=jax.ShapeDtypeStruct(vectors.shape, F32),
        in_specs=[any_spec] * 3,
        out_specs=pl.BlockSpec(memory_space=pltpu.VMEM),
        scratch_shapes=[
            vmem((2, 8, 32, 512), F32),
            vmem((8, 2, 32, 256), F32),
            vmem((512, 128), F32),
            vmem((160, 512), BF16),
            vmem((160, 512), BF16),
            vmem((2, YL, 5, 8, 128), F32),
            vmem((2, YL, 4, 8, 128), F32),
            vmem((YL, 5, 8, 128), F32),
            vmem((YL, 4, 8, 128), F32),
            vmem((YL, 5, 8, 128), F32),
            vmem((YL, 4, 8, 128), F32),
            vmem((YL - 1, 5, 8, 128), F32),
            vmem((YL - 1, 4, 8, 128), F32),
            vmem((5, 8, 128), F32),
            vmem((4, 8, 128), F32),
            vmem((NZ - 1, 5, 8, 128), F32),
            vmem((NZ - 1, 4, 8, 128), F32),
            vmem((2, YL, 4, 8, 128), F32),
            vmem((2, YL, 4, 8, 128), F32),
            vmem((2, 8, YL, 8, 128), F32),
            vmem((512, 256), BF16),
            vmem((512, 256), BF16),
            vmem((512, 256), BF16),
            vmem((512, 256), BF16),
            pltpu.SemaphoreType.DMA((4,)),
            pltpu.SemaphoreType.DMA((N_COPIES,)),
            pltpu.SemaphoreType.DMA((N_COPIES,)),
        ],
        compiler_params=pltpu.CompilerParams(
            collective_id=0, has_side_effects=True, vmem_limit_bytes=60 * 2**20
        ),
        cost_estimate=pl.CostEstimate(flops=500_000_000, bytes_accessed=2_000_000, transcendentals=0),
        name="reflect",
    )(v_t, t_t, vectors)


def solution(mesh):
    return jax.shard_map(
        on_device,
        mesh=mesh,
        in_specs=(P("row", "col"), P(None, "row", "col"), P(None, None, "col")),
        out_specs=P("row", "col"),
        check_vma=False,
    )
```

time: 164 us -> 56.5 us (0.34)
  blocking collectives: 126 us -> 0 us
  Pallas kernels: 0 us -> 54.7 us
  starting transfers between devices: 20.6 us -> 0 us
  waiting for transfers between devices: 9.97 us -> 0 us
  matrix products: 4.25 us -> 0 us
    all_gather x2 -> x0, blocking collectives: 85.3 us -> none  [turned_gather(): lax.all_gather(both, axis, axis=0, tiled=True)]
    pallas_call x0 -> x1, Pallas kernels: none -> 54.7 us  [on_device(): pl.pallas_call(kernel, out_shape=jax.ShapeDtypeStruct(vectors.shape, F32)...]
    all_to_all x2 -> x0, blocking collectives: 40.7 us -> none  [the longest x1 26.1 us: summed_on_arrival(): tiles = lax.all_to_all(split_up(value, dim, length), axis, 0, 0, tiled=True)]
    all_to_all x2 -> x0, starting transfers between devices: 20.6 us -> none  [the longest x1 15.6 us: summed_on_arrival(): tiles = lax.all_to_all(split_up(value, dim, length), axis, 0, 0, tiled=True)]
    all_to_all x2 -> x0, waiting for transfers between devices: 9.97 us -> none  [the longest x1 9.97 us: summed_on_arrival(): tiles = lax.all_to_all(split_up(value, dim, length), axis, 0, 0, tiled=True)]
    dot_general x6 -> x0, matrix products: 4.25 us -> none  [the longest x2 2.7 us: on_device(): lax.dot_general(blockv, reflect_t, (((1,), (1,)), ((), ())), precision=la...]
  transfers between devices with their start and end apart: 2 -> 0, of which waited for: 1 -> 0; matrix products, arithmetic and copies ran while one was open for 0% -> 0% of each run, Pallas kernels for 0% -> 0%
where the time goes in v1:
time: 56.5 us; the launch traced here: 56.3 us
  Pallas kernels  54.7 us (97%)
  local copies, waits for them, and re-layouts  1.67 us (3%)
    pallas_call x1, Pallas kernels, on_device(): pl.pallas_call(kernel, out_shape=jax.ShapeDtypeStruct(vectors.shape, F32)...  54.7 us
    unnamed x1, local copies, waits for them, and re-layouts  1.67 us

profile of v1, /device:TPU:1, one launch (start us, length us, event | category | flops | bytes accessed | tf_op | source)
XLA Modules:
  0.0 56.3 jit_solution(17260673138121782692)
XLA Ops:
  0.0 54.7 %reflect.1 = f32[512,128]{1,0:T(8,128)} custom-call(f32[2,32,512]{2,1,0:T(8,128)} %bitcast.2, f32[2,32,256]{2,1,0:T(8,128)} %bitcast.3, f32[512,128]{1,0:T(8,128)} %c_in.1), custom_call_target="tpu_custom_call" | custom-call | flops 500000000 | bytes 2000000 | tf_op jit(solution)/shard_map/reflect/pallas_call | solution.py:234
  54.7 1.7 %copy.5 = f32[512,128]{1,0:T(8,128)} copy(f32[512,128]{1,0:T(8,128)} %reflect.1) | data formatting | bytes 524288

commit v2 on v0

v2 whole, which is shorter than its diff:
```python
import functools

import jax
import jax.numpy as jnp
from jax import lax
from jax.experimental import pallas as pl
from jax.experimental.pallas import tpu as pltpu
from jax.sharding import PartitionSpec as P

MESH = pl.DeviceIdType.MESH
F32 = jnp.float32
BF16 = jnp.bfloat16
YL, NZ, CORES = 4, 8, 2
YH, NX = 2, 4
NT = (((1,), (1,)), ((), ()))
NN = (((1,), (0,)), ((), ()))


def split(value):
    high = value.astype(BF16)
    return high, (value - high.astype(F32)).astype(BF16)


def dot3(a, b, dims):
    def one(left, right):
        return lax.dot_general(left, right, dims, preferred_element_type=F32)

    return one(a[0], b[0]) + (one(a[0], b[1]) + one(a[1], b[0]))


class Copies:
    def __init__(self, send, recv):
        self.send, self.recv, self.used, self.open = send, recv, 0, []

    def start(self, src, dst, device):
        at = self.used
        self.used += 1
        copy = pltpu.make_async_remote_copy(
            src_ref=src,
            dst_ref=dst,
            send_sem=self.send.at[at],
            recv_sem=self.recv.at[at],
            device_id=device,
            device_id_type=MESH,
        )
        copy.start()
        self.open.append(copy)
        return copy

    def finish(self):
        for copy in self.open:
            copy.wait_send()


N_COPIES = 114
Z_ORDER = (4, 3, 5, 2, 6, 1, 7)
OTHERS = tuple((dyl, dc) for dyl in (3, 2, 1, 0) for dc in (1, 0) if dyl or dc)
NEAR, FAR = 0, 1
SETS = (((0, NEAR), (1, NEAR)), ((0, FAR),), ((1, FAR),))
DIRECT = (False, True, True)


def kernel(sets, direct, v_in, t_in, c_in, out_ref, *scratch):
    (
        vt, tt, c_v, lhs_h, lhs_l, w1h, w1l, v0h, v0l, r0h, r0l, gf, local_sem, send_sem, recv_sem,
    ), per_set = scratch[:15], scratch[15:]
    parts = [per_set[7 * i : 7 * i + 7] for i in range(len(sets))]
    row, col = lax.axis_index("row"), lax.axis_index("col")
    core, z, yl = lax.rem(row, 2), lax.rem(row // 2, NZ), row // (2 * NZ)
    x, yh = lax.rem(col, NX), col // NX
    cores = [core, 1 - core]
    zs = [lax.rem(z + d, NZ) for d in range(NZ)]
    yls = [lax.rem(yl + d, YL) for d in range(YL)]
    xs = [lax.rem(x + d, NX) for d in range(NX)]
    halves = [yh, 1 - yh]
    other_col = halves[FAR] * NX + x

    def at(dc=0, dz=0, dyl=0, dx=0, dyh=0):
        return (yls[dyl] * (2 * NZ) + zs[dz] * 2 + cores[dc], halves[dyh] * NX + xs[dx])

    load_v = [pltpu.make_async_copy(v_in.at[b], vt.at[b, col], local_sem.at[b]) for b in range(2)]
    load_c = pltpu.make_async_copy(c_in, c_v, local_sem.at[2])
    load_t = pltpu.make_async_copy(t_in.at[core], tt.at[core, col], local_sem.at[3])
    for load in (*load_v, load_c, load_t):
        load.start()

    barrier = pltpu.get_barrier_semaphore()
    partners = [at(dyh=1)] + [at(dx=d) for d in (2, 1, 3)] + [at(dz=d) for d in Z_ORDER]
    partners += [at(dyl=dyl, dc=dc) for dyl, dc in OTHERS]
    for device in partners:
        pl.semaphore_signal(barrier, inc=1, device_id=device, device_id_type=MESH)
    for load in load_v:
        load.wait()
    pl.semaphore_wait(barrier, len(partners))

    copies = Copies(send_sem, recv_sem)
    going = {}

    def wait(*names):
        for name in names:
            for copy in going.pop(name, ()):
                copy.wait_recv()

    def along_x(ref):
        return [copies.start(ref, ref, at(dx=d)) for d in (2, 1, 3)]

    def to_partner(ref):
        return [copies.start(ref, ref, at(dyh=1))]

    def send_x0():
        going["x0"] = along_x(vt.at[0, col])

    def send_x1():
        going["x1"] = along_x(vt.at[1, col])

    def send_y0():
        going["y0"] = to_partner(vt.at[0, col])

    def send_y1():
        going["y1"] = to_partner(vt.at[1, col])

    def send_yt():
        load_t.wait()
        going["yt"] = to_partner(tt.at[core, col])

    def turn_own():
        load_c.wait()
        for part in range(2):
            high, low = split(jnp.transpose(c_v[pl.ds(256 * part, 256), :]))
            lhs_h[0:128, 256 * part : 256 * (part + 1)] = high
            lhs_l[0:128, 256 * part : 256 * (part + 1)] = low

    def relay0():
        wait("y0")
        going["r0"] = along_x(vt.at[0, other_col])

    def relay1():
        wait("y1")
        going["r1"] = along_x(vt.at[1, other_col])

    def gram_rows():
        for half in range(2):
            first = 128 + 32 * half
            high, low = split(vt[1, half * NX + x])
            lhs_h[first : first + 32, :] = high
            lhs_l[first : first + 32, :] = low

    def relay_t():
        wait("yt")
        going["rt"] = along_x(tt.at[core, col]) + along_x(tt.at[core, other_col])

    def swap_t():
        wait("rt")
        going["ct"] = [copies.start(tt.at[core], tt.at[core], at(dc=1))]

    def mul(i):
        pp, rs = parts[i][:2]
        grams = 2 * len(sets[i])
        for n, (b, half) in enumerate(sets[i]):
            wait(("x0", "x1")[b] if half == NEAR else ("r0", "r1")[b])
            rows = 192 if (b, half) == (0, NEAR) else 128
            blockv = split(vt[b, pl.ds(halves[half] * NX, NX)].reshape(128, 512))
            value = dot3((lhs_h[0:rows, :], lhs_l[0:rows, :]), blockv, NT)
            for e in range(2 * YL):
                c, y = divmod(e, YL)
                pp[c, y, 2 * n : 2 * n + 2] = value[16 * e : 16 * e + 16].reshape(2, 8, 128)
                if rows == 192:
                    pp[c, y, grams] = value[128 + 8 * e : 136 + 8 * e]
        if direct[i]:
            going["y", i] = [
                copies.start(pp.at[cores[dc], yls[dyl]], parts[i][3].at[j], at(dyl=dyl, dc=dc))
                for j, (dyl, dc) in enumerate(OTHERS)
            ]
        else:
            going["core", i] = [copies.start(pp.at[1 - core], rs, at(dc=1))]

    def down(i):
        if direct[i]:
            return
        pp, rs, held, yr, _, _, _ = parts[i]
        wait(("core", i))
        held[...] = pp[core] + rs[...]
        going["y", i] = [
            copies.start(held.at[yls[d]], yr.at[d - 1], at(dyl=d)) for d in (3, 2, 1)
        ]

    def around(i):
        pp, _, held, yr, mine, zr, _ = parts[i]
        wait(("y", i))
        if direct[i]:
            total = pp[core, yl]
            for j in range(len(OTHERS)):
                total = total + yr[j]
            mine[...] = total
        else:
            mine[...] = held[yl] + yr[0] + (yr[1] + yr[2])
        going["z", i] = [copies.start(mine, zr.at[d - 1], at(dz=d)) for d in Z_ORDER]

    def up(i):
        mine, zr, pf = parts[i][4:]
        wait(("z", i))
        total = mine[...]
        for d in range(NZ - 1):
            total = total + zr[d]
        grams = 2 * len(sets[i])
        pf[core, yl] = total[0:grams]
        sent = pf.at[core, yl]
        if direct[i]:
            going["over", i] = [copies.start(sent, sent, at(dyl=dyl, dc=dc)) for dyl, dc in OTHERS]
        else:
            going["up", i] = [copies.start(sent, sent, at(dyl=d)) for d in (3, 2, 1)]
            going["over", i] = [copies.start(sent, sent, at(dc=1))]
        if (0, NEAR) in sets[i]:
            gf[core, yh, x, yl] = total[grams]
            place = gf.at[core, yh, x, yl]
            going["g"] = [
                copies.start(place, place, at(dx=dx, dyl=dyl, dyh=dyh))
                for dyh in (1, 0)
                for dyl in (3, 2, 1, 0)
                for dx in (2, 1, 3, 0)
                if dx or dyl or dyh
            ]

    def over(i):
        if direct[i]:
            return
        pf = parts[i][6]
        for d, copy in zip((3, 2, 1), going.pop(("up", i))):
            copy.wait_recv()
            came = pf.at[core, lax.rem(yl + YL - d, YL)]
            going["over", i].append(copies.start(came, came, at(dc=1)))

    def pre0():
        wait("r0")
        for half in range(2):
            block = vt[0, pl.ds(halves[half] * NX, NX)].reshape(128, 512)
            high, low = split(jnp.transpose(block))
            v0h[:, 128 * half : 128 * (half + 1)] = high
            v0l[:, 128 * half : 128 * (half + 1)] = low

    def factor(b):
        both = [tt[b, pl.ds(half * NX, NX)].reshape(128, 256) for half in halves]
        return split(jnp.concatenate(both, axis=0))

    def pre1():
        wait("r1", "ct")
        v1 = split(jnp.transpose(vt[1].reshape(256, 512)))
        w1h[...], w1l[...] = split(dot3(v1, factor(1), NT))

    def products(b):
        found = {}
        for i, pieces in enumerate(sets):
            for n, piece in enumerate(pieces):
                found[piece] = parts[i][6][:, :, 2 * n : 2 * n + 2].reshape(128, 128)
        return jnp.concatenate([found[b, NEAR], found[b, FAR]], axis=1)

    def gram_over():
        wait("g")
        going["gc"] = [copies.start(gf.at[core], gf.at[core], at(dc=1))]

    def gram(half):
        tiles = [gf[k1, halves[half], g].reshape(32, 128) for k1 in halves for g in range(NX)]
        return jnp.concatenate(tiles, axis=0)

    def last():
        wait(*(("over", i) for i in range(len(sets)) if any(b == 0 for b, _ in sets[i])))
        high, low = split(dot3(split(products(0)), factor(0), NN))
        for h in range(2):
            r0h[h] = high[:, 128 * h : 128 * (h + 1)]
            r0l[h] = low[:, 128 * h : 128 * (h + 1)]
        r0 = tuple(jnp.concatenate([r[half] for half in halves], axis=1) for r in (r0h, r0l))
        c_v[...] = c_v[...] - dot3((v0h[...], v0l[...]), r0, NT)
        wait("gc")
        moved = dot3(r0, split(jnp.concatenate([gram(0), gram(1)], axis=1)), NT)
        wait(*(("over", i) for i in range(len(sets))))
        rest = split(products(1) - moved)
        out_ref[...] = c_v[...] - dot3((w1h[...], w1l[...]), rest, NT)

    send_y0()
    send_x0()
    send_y1()
    send_x1()
    send_yt()
    turn_own()
    relay0()
    relay1()
    gram_rows()
    mul(0)
    down(0)
    mul(1)
    around(0)
    mul(2)
    around(1)
    relay_t()
    up(0)
    around(2)
    pre0()
    up(1)
    over(0)
    up(2)
    swap_t()
    pre1()
    gram_over()
    last()
    copies.finish()


def on_device(vectors, householder, tfactors):
    v_t = jnp.swapaxes(householder, 1, 2)
    t_t = jnp.swapaxes(tfactors, 1, 2)
    anywhere = pl.BlockSpec(memory_space=pl.ANY)
    vmem = pltpu.VMEM
    tiles = lambda *shape: vmem((*shape, 8, 128), F32)
    scratch = [
        vmem((2, 8, 32, 512), F32),
        vmem((2, 8, 32, 256), F32),
        vmem((512, 128), F32),
        vmem((192, 512), BF16),
        vmem((192, 512), BF16),
        vmem((512, 256), BF16),
        vmem((512, 256), BF16),
        vmem((512, 256), BF16),
        vmem((512, 256), BF16),
        vmem((2, 128, 128), BF16),
        vmem((2, 128, 128), BF16),
        tiles(2, 2, NX, YL),
        pltpu.SemaphoreType.DMA((4,)),
        pltpu.SemaphoreType.DMA((N_COPIES,)),
        pltpu.SemaphoreType.DMA((N_COPIES,)),
    ]
    for pieces in SETS:
        n = 2 * len(pieces)
        with_gram = n + ((0, NEAR) in pieces)
        scratch += [
            tiles(2, YL, with_gram), tiles(YL, with_gram), tiles(YL, with_gram), tiles(7, with_gram),
            tiles(with_gram), tiles(NZ - 1, with_gram), tiles(2, YL, n),
        ]
    return pl.pallas_call(
        functools.partial(kernel, SETS, DIRECT),
        out_shape=pltpu.VMEM(vectors.shape, F32),
        in_specs=[anywhere] * 3,
        out_specs=pl.BlockSpec(memory_space=pltpu.VMEM),
        scratch_shapes=scratch,
        compiler_params=pltpu.CompilerParams(
            collective_id=0, has_side_effects=True, vmem_limit_bytes=61440 * 1024
        ),
        cost_estimate=pl.CostEstimate(flops=500_000_000, bytes_accessed=2_000_000, transcendentals=0),
        name="reflect",
    )(v_t, t_t, vectors)


def solution(mesh):
    return jax.shard_map(
        on_device,
        mesh=mesh,
        in_specs=(P("row", "col"), P(None, "row", "col"), P(None, None, "col")),
        out_specs=P("row", "col"),
        check_vma=False,
    )
```

time: 164 us -> 50.3 us (0.31)
  blocking collectives: 126 us -> 0 us
  Pallas kernels: 0 us -> 49.4 us
  starting transfers between devices: 20.6 us -> 0 us
  waiting for transfers between devices: 9.97 us -> 0 us
  matrix products: 4.25 us -> 0 us
  local copies, waits for them, and re-layouts: 2.75 us -> 0.71 us
    all_gather x2 -> x0, blocking collectives: 85.3 us -> none  [turned_gather(): lax.all_gather(both, axis, axis=0, tiled=True)]
    pallas_call x0 -> x1, Pallas kernels: none -> 49.4 us  [on_device(): pl.pallas_call(functools.partial(kernel, SETS, DIRECT), out_shape=pltpu.V...]
    all_to_all x2 -> x0, blocking collectives: 40.7 us -> none  [the longest x1 26.1 us: summed_on_arrival(): tiles = lax.all_to_all(split_up(value, dim, length), axis, 0, 0, tiled=True)]
    all_to_all x2 -> x0, starting transfers between devices: 20.6 us -> none  [the longest x1 15.6 us: summed_on_arrival(): tiles = lax.all_to_all(split_up(value, dim, length), axis, 0, 0, tiled=True)]
    all_to_all x2 -> x0, waiting for transfers between devices: 9.97 us -> none  [the longest x1 9.97 us: summed_on_arrival(): tiles = lax.all_to_all(split_up(value, dim, length), axis, 0, 0, tiled=True)]
    dot_general x6 -> x0, matrix products: 4.25 us -> none  [the longest x2 2.7 us: on_device(): lax.dot_general(blockv, reflect_t, (((1,), (1,)), ((), ())), precision=la...]
  transfers between devices with their start and end apart: 2 -> 0, of which waited for: 1 -> 0; matrix products, arithmetic and copies ran while one was open for 0% -> 0% of each run, Pallas kernels for 0% -> 0%
where the time goes in v2:
time: 50.3 us; the launch traced here: 50.1 us
  Pallas kernels  49.4 us (98%)
  local copies, waits for them, and re-layouts  0.71 us (1%)
    pallas_call x1, Pallas kernels, on_device(): pl.pallas_call(functools.partial(kernel, SETS, DIRECT), out_shape=pltpu.V...  49.4 us

profile of v2, /device:TPU:1, one launch (start us, length us, event | category | flops | bytes accessed | tf_op | source)
XLA Modules:
  0.0 50.1 jit_solution(17296777613234517102)
XLA Ops:
  0.0 49.4 %reflect.1 = f32[512,128]{1,0:T(8,128)S(1)} custom-call(f32[2,32,512]{2,1,0:T(8,128)} %bitcast.2, f32[2,32,256]{2,1,0:T(8,128)} %bitcast.3, f32[512,128]{1,0:T(8,128)} %c_in.1), custom_call_target="tpu_custom_call" | custom-call | flops 500000000 | bytes 2000000 | tf_op jit(solution)/shard_map/reflect/pallas_call | solution.py:338
  49.4 0.7 %copy.5 = f32[512,128]{1,0:T(8,128)} copy(f32[512,128]{1,0:T(8,128)S(1)} %reflect.1) | data formatting | bytes 524288

commit v3 on v2

--- a/solution.py
+++ b/solution.py
@@ -52,12 +52,13 @@
             copy.wait_send()
 
 
-N_COPIES = 114
+N_COPIES = 138
 Z_ORDER = (4, 3, 5, 2, 6, 1, 7)
 OTHERS = tuple((dyl, dc) for dyl in (3, 2, 1, 0) for dc in (1, 0) if dyl or dc)
 NEAR, FAR = 0, 1
-SETS = (((0, NEAR), (1, NEAR)), ((0, FAR),), ((1, FAR),))
-DIRECT = (False, True, True)
+GRAM = (1, NEAR)
+SETS = (((0, NEAR),), ((1, NEAR),), ((0, FAR),), ((1, FAR),))
+DIRECT = (True, True, True, True)
 
 
 def kernel(sets, direct, v_in, t_in, c_in, out_ref, *scratch):
@@ -158,14 +159,18 @@
         grams = 2 * len(sets[i])
         for n, (b, half) in enumerate(sets[i]):
             wait(("x0", "x1")[b] if half == NEAR else ("r0", "r1")[b])
-            rows = 192 if (b, half) == (0, NEAR) else 128
             blockv = split(vt[b, pl.ds(halves[half] * NX, NX)].reshape(128, 512))
-            value = dot3((lhs_h[0:rows, :], lhs_l[0:rows, :]), blockv, NT)
+            value = dot3((lhs_h[0:128, :], lhs_l[0:128, :]), blockv, NT)
             for e in range(2 * YL):
                 c, y = divmod(e, YL)
                 pp[c, y, 2 * n : 2 * n + 2] = value[16 * e : 16 * e + 16].reshape(2, 8, 128)
-                if rows == 192:
-                    pp[c, y, grams] = value[128 + 8 * e : 136 + 8 * e]
+        if GRAM in sets[i]:
+            wait("x0")
+            blockv = split(vt[0, pl.ds(yh * NX, NX)].reshape(128, 512))
+            value = dot3((lhs_h[128:192, :], lhs_l[128:192, :]), blockv, NT)
+            for e in range(2 * YL):
+                c, y = divmod(e, YL)
+                pp[c, y, grams] = value[8 * e : 8 * e + 8]
         if direct[i]:
             going["y", i] = [
                 copies.start(pp.at[cores[dc], yls[dyl]], parts[i][3].at[j], at(dyl=dyl, dc=dc))
@@ -210,7 +215,7 @@
         else:
             going["up", i] = [copies.start(sent, sent, at(dyl=d)) for d in (3, 2, 1)]
             going["over", i] = [copies.start(sent, sent, at(dc=1))]
-        if (0, NEAR) in sets[i]:
+        if GRAM in sets[i]:
             gf[core, yh, x, yl] = total[grams]
             place = gf.at[core, yh, x, yl]
             going["g"] = [
@@ -283,23 +288,24 @@
     send_yt()
     turn_own()
     relay0()
+    mul(0)
     relay1()
     gram_rows()
-    mul(0)
-    down(0)
     mul(1)
     around(0)
     mul(2)
     around(1)
-    relay_t()
+    mul(3)
     up(0)
     around(2)
+    relay_t()
+    up(1)
+    around(3)
     pre0()
-    up(1)
-    over(0)
     up(2)
     swap_t()
     pre1()
+    up(3)
     gram_over()
     last()
     copies.finish()
@@ -330,7 +336,7 @@
     ]
     for pieces in SETS:
         n = 2 * len(pieces)
-        with_gram = n + ((0, NEAR) in pieces)
+        with_gram = n + (GRAM in pieces)
         scratch += [
             tiles(2, YL, with_gram), tiles(YL, with_gram), tiles(YL, with_gram), tiles(7, with_gram),
             tiles(with_gram), tiles(NZ - 1, with_gram), tiles(2, YL, n),
@@ -342,7 +348,7 @@
         out_specs=pl.BlockSpec(memory_space=pltpu.VMEM),
         scratch_shapes=scratch,
         compiler_params=pltpu.CompilerParams(
-            collective_id=0, has_side_effects=True, vmem_limit_bytes=61440 * 1024
+            collective_id=0, has_side_effects=True, vmem_limit_bytes=60 * 2**20
         ),
         cost_estimate=pl.CostEstimate(flops=500_000_000, bytes_accessed=2_000_000, transcendentals=0),
         name="reflect",

time: 50.3 us -> 48.8 us (0.970)
  Pallas kernels: 49.4 us -> 48 us
    pallas_call x1, Pallas kernels: 49.4 us -> 48 us  [on_device(): pl.pallas_call(functools.partial(kernel, SETS, DIRECT), out_shape=pltpu.V...]
where the time goes in v3:
time: 48.8 us; the launch traced here: 48.7 us
  Pallas kernels  48 us (98%)
  local copies, waits for them, and re-layouts  0.71 us (1%)
    pallas_call x1, Pallas kernels, on_device(): pl.pallas_call(functools.partial(kernel, SETS, DIRECT), out_shape=pltpu.V...  48 us

profile of v3, /device:TPU:1, one launch (start us, length us, event | category | flops | bytes accessed | tf_op | source)
XLA Modules:
  0.0 48.7 jit_solution(3071557728687403937)
XLA Ops:
  0.0 48.0 %reflect.1 = f32[512,128]{1,0:T(8,128)S(1)} custom-call(f32[2,32,512]{2,1,0:T(8,128)} %bitcast.2, f32[2,32,256]{2,1,0:T(8,128)} %bitcast.3, f32[512,128]{1,0:T(8,128)} %c_in.1), custom_call_target="tpu_custom_call" | custom-call | flops 500000000 | bytes 2000000 | tf_op jit(solution)/shard_map/reflect/pallas_call | solution.py:344
  48.0 0.7 %copy.5 = f32[512,128]{1,0:T(8,128)} copy(f32[512,128]{1,0:T(8,128)S(1)} %reflect.1) | data formatting | bytes 524288

commit v4 on v3

--- a/solution.py
+++ b/solution.py
@@ -103,7 +103,7 @@
                 copy.wait_recv()
 
     def along_x(ref):
-        return [copies.start(ref, ref, at(dx=d)) for d in (2, 1, 3)]
+        return [copies.start(ref, ref, at(dx=d)) for d in (1, 3, 2)]
 
     def to_partner(ref):
         return [copies.start(ref, ref, at(dyh=1))]

time: 48.8 us -> 48.6 us (level)
  no operation moved by 1% of the time
where the time goes in v4:
time: 48.6 us; the launch traced here: 48.5 us
  Pallas kernels  47.8 us (98%)
  local copies, waits for them, and re-layouts  0.71 us (1%)
    pallas_call x1, Pallas kernels, on_device(): pl.pallas_call(functools.partial(kernel, SETS, DIRECT), out_shape=pltpu.V...  47.8 us

profile of v4, /device:TPU:1, one launch (start us, length us, event | category | flops | bytes accessed | tf_op | source)
XLA Modules:
  0.0 48.5 jit_solution(8171991884861793737)
XLA Ops:
  0.0 47.8 %reflect.1 = f32[512,128]{1,0:T(8,128)S(1)} custom-call(f32[2,32,512]{2,1,0:T(8,128)} %bitcast.2, f32[2,32,256]{2,1,0:T(8,128)} %bitcast.3, f32[512,128]{1,0:T(8,128)} %c_in.1), custom_call_target="tpu_custom_call" | custom-call | flops 500000000 | bytes 2000000 | tf_op jit(solution)/shard_map/reflect/pallas_call | solution.py:344
  47.8 0.7 %copy.5 = f32[512,128]{1,0:T(8,128)} copy(f32[512,128]{1,0:T(8,128)S(1)} %reflect.1) | data formatting | bytes 524288
